TPU v7x, 32 devices: a whole 2x2x4 slice. The times are simulated.
32 devices in a mesh: dp: 8 (over z, x), seq: 4 (over y, core).
Axes of the slice: x: 2, y: 2, z: 4, core: 2. Of those that a mesh axis runs over, the one named last changes fastest.
Arguments:
- hidden_states: bfloat16 [8, 512, 4096], P('dp', 'seq'), may hold values from -6 to 6
- queries: bfloat16 [8, 512, 4096], P('dp', 'seq'), may hold values from -20 to 20
- key_states: bfloat16 [8, 512, 512], P('dp', 'seq'), may hold values from -6 to 6
- context_grad: bfloat16 [8, 512, 4096], P('dp', 'seq'), may hold values from -6 to 6
- doc_lengths: int32 [8, 16], P('dp'), may hold values from 1 to 64, 512 in all within a row
- value_weight: bfloat16 [4096, 512], P('dp'), may hold values from -0.09375 to 0.09375
Outputs:
- hidden_grad: bfloat16 [8, 512, 4096], P('dp', 'seq')
- query_grad: bfloat16 [8, 512, 4096], P('dp', 'seq')
- key_grad: bfloat16 [8, 512, 512], P('dp', 'seq')
- value_weight_grad: float32 [4096, 512], P(('dp', 'seq'))
Inputs may be any that keep to these rules, and one draw needn't show every extreme that they name: `doc_lengths`: row s holds the lengths of the 16 documents of sequence s in order; they sum to 512.
All inputs are finite; a program needn't handle non-finite values.
Results may differ from a plain program's by a relative error of at most 0.011.
Values may be sent and summed in bfloat16 or wider, within the bound.
A program may use at most 128 MiB of HBM per device.

v0:
```python
import jax
import jax.numpy as jnp
from jax import lax
from jax.sharding import PartitionSpec as P

HD = 128
far_negative = -1e30


def segment_ids(lengths_row, length):
    doc_ends = jnp.cumsum(lengths_row)
    positions = jnp.arange(length, dtype=jnp.int32)
    return jnp.sum((positions[:, None] >= doc_ends[None, :]).astype(jnp.int32), axis=1)


def attend(query_all, key_all, value_all, grad_all, segment):
    length, head_count, head_width = query_all.shape
    row_block = min(length, max(512, length // 8))
    longest_doc = length // 8
    score_scale = head_width ** (-0.5)
    positions = jnp.arange(length, dtype=jnp.int32)
    key_acc = jnp.zeros((length, head_count, head_width), jnp.float32)
    value_acc = jnp.zeros((length, head_count, head_width), jnp.float32)
    query_parts = []
    for row_start in range(0, length, row_block):
        row_end = row_start + row_block
        key_start = max(0, row_start - longest_doc)
        query_rows = query_all[row_start:row_end]
        grad_rows = grad_all[row_start:row_end]
        key_rows = key_all[key_start:row_end]
        value_rows = value_all[key_start:row_end]
        allowed = (positions[None, key_start:row_end] <= positions[row_start:row_end, None]) & (
            segment[None, key_start:row_end] == segment[row_start:row_end, None]
        )
        scores = (
            jnp.einsum("ihd,jhd->hij", query_rows, key_rows, preferred_element_type=jnp.float32)
            * score_scale
        )
        scores = jnp.where(allowed[None], scores, far_negative)
        row_peak = jnp.max(scores, axis=-1, keepdims=True)
        exponent = jnp.exp(scores - row_peak)
        softmax_weights = exponent / jnp.sum(exponent, axis=-1, keepdims=True)
        weights_low = softmax_weights.astype(jnp.bfloat16)
        attended = jnp.einsum(
            "hij,jhd->ihd", weights_low, value_rows, preferred_element_type=jnp.float32
        )
        row_delta = jnp.sum(grad_rows.astype(jnp.float32) * attended, axis=-1)
        softmax_grad = jnp.einsum(
            "ihd,jhd->hij", grad_rows, value_rows, preferred_element_type=jnp.float32
        )
        score_grad = softmax_weights * (softmax_grad - jnp.transpose(row_delta)[:, :, None])
        score_low = score_grad.astype(jnp.bfloat16)
        query_parts.append(
            (
                jnp.einsum("hij,jhd->ihd", score_low, key_rows, preferred_element_type=jnp.float32)
                * score_scale
            ).astype(jnp.bfloat16)
        )
        key_acc = key_acc.at[key_start:row_end].add(
            jnp.einsum("hij,ihd->jhd", score_low, query_rows, preferred_element_type=jnp.float32)
            * score_scale
        )
        value_acc = value_acc.at[key_start:row_end].add(
            jnp.einsum("hij,ihd->jhd", weights_low, grad_rows, preferred_element_type=jnp.float32)
        )
    return (jnp.concatenate(query_parts, axis=0), key_acc, value_acc)


def body(hidden_states, queries, key_states, context_grad, doc_lengths, value_weight):
    tokens = hidden_states.shape[1]
    rows_here = hidden_states[0]
    heads_total = queries.shape[2] // HD
    kv_heads = key_states.shape[2] // HD
    group_size = heads_total // kv_heads
    columns = rows_here
    values = jnp.dot(
        columns,
        lax.all_gather(value_weight, "dp", axis=0, tiled=True),
        preferred_element_type=jnp.float32,
    ).astype(jnp.bfloat16)
    query_heads = queries[0].reshape(tokens, heads_total, HD)
    grad_heads = context_grad[0].reshape(tokens, heads_total, HD)
    query_all, grad_all = (
        lax.all_to_all(query_heads, "seq", split_axis=1, concat_axis=0, tiled=True),
        lax.all_to_all(grad_heads, "seq", split_axis=1, concat_axis=0, tiled=True),
    )
    length = query_all.shape[0]
    key_three = key_states[0].reshape(tokens, kv_heads, HD)
    value_three = values.reshape(tokens, kv_heads, HD)
    segment = segment_ids(doc_lengths[0], length)
    key_all, value_all = (
        lax.all_to_all(
            jnp.repeat(key_three, group_size, axis=1),
            "seq",
            split_axis=1,
            concat_axis=0,
            tiled=True,
        ),
        lax.all_to_all(
            jnp.repeat(value_three, group_size, axis=1),
            "seq",
            split_axis=1,
            concat_axis=0,
            tiled=True,
        ),
    )
    query_back, key_back, value_back = attend(query_all, key_all, value_all, grad_all, segment)
    key_home, value_home = (
        lax.all_to_all(
            key_back.astype(jnp.bfloat16), "seq", split_axis=0, concat_axis=1, tiled=True
        ).astype(key_back.dtype),
        lax.all_to_all(
            value_back.astype(jnp.bfloat16), "seq", split_axis=0, concat_axis=1, tiled=True
        ).astype(value_back.dtype),
    )
    key_sum = jnp.sum(key_home.reshape(tokens, kv_heads, group_size, HD), axis=2)
    value_sum = jnp.sum(value_home.reshape(tokens, kv_heads, group_size, HD), axis=2)
    query_home = lax.all_to_all(query_back, "seq", split_axis=0, concat_axis=1, tiled=True)
    value_low = value_sum.reshape(tokens, kv_heads * HD).astype(jnp.bfloat16)
    hidden_grad = jnp.einsum(
        "tc,rc->tr",
        value_low,
        lax.all_gather(value_weight, "dp", axis=0, tiled=True),
        preferred_element_type=jnp.float32,
    )
    columns = rows_here
    weight_grad = lax.psum_scatter(
        jnp.einsum("tr,tc->rc", columns, value_low, preferred_element_type=jnp.float32),
        ("dp", "seq"),
        scatter_dimension=0,
        tiled=True,
    )
    return (
        hidden_grad.astype(jnp.bfloat16)[None],
        query_home.reshape(tokens, heads_total * HD)[None],
        key_sum.reshape(tokens, kv_heads * HD).astype(jnp.bfloat16)[None],
        weight_grad,
    )


def solution(mesh):
    return jax.shard_map(
        body,
        mesh=mesh,
        in_specs=(
            P("dp", "seq", None),
            P("dp", "seq", None),
            P("dp", "seq", None),
            P("dp", "seq", None),
            P("dp", None),
            P("dp", None),
        ),
        out_specs=(
            P("dp", "seq", None),
            P("dp", "seq", None),
            P("dp", "seq", None),
            P(("dp", "seq"), None),
        ),
        check_vma=False,
    )
```

profile of v0, /device:TPU:0, one launch (start us, length us, event | category | flops | bytes accessed | tf_op | source)
XLA Modules:
  0.0 270.5 jit_solution(17113018626907057216)
XLA Ops:
  11.7 4.2 %all-to-all-start = ((bf16[128,32,128]{2,0,1:T(8,128)(2,1)}), bf16[128,32,128]{2,0,1:T(8,128)(2,1)S(1)}, u32[]{:S(2)}, u32[]{:S(2)}) async-start(bf16[128,32,128]{2,0,1:T(8,128)(2,1)} %copy.94), calls=%async_computation | async-start | bytes 2097152 | tf_op jit(solution)/shard_map/all_to_all | solution.py:84
  16.0 14.4 %all-to-all-done = bf16[128,32,128]{2,0,1:T(8,128)(2,1)S(1)} async-done(((bf16[128,32,128]{2,0,1:T(8,128)(2,1)}), bf16[128,32,128]{2,0,1:T(8,128)(2,1)S(1)}, u32[]{:S(2)}, u32[]{:S(2)}) %all-to-all-start) | async-done | bytes 1048608 | tf_op jit(solution)/shard_map/all_to_all | solution.py:84
  31.6 3.7 %all-to-all-start.1 = ((bf16[128,32,128]{2,0,1:T(8,128)(2,1)}), bf16[128,32,128]{2,0,1:T(8,128)(2,1)S(1)}, u32[]{:S(2)}, u32[]{:S(2)}) async-start(bf16[128,32,128]{2,0,1:T(8,128)(2,1)} %bitcast.84), calls=%async_computation.1 | async-start | bytes 2097152 | tf_op jit(solution)/shard_map/all_to_all | solution.py:92
  35.3 2.3 copy.100
  37.5 2.3 copy.101
  39.8 9.9 %all-to-all-done.1 = bf16[128,32,128]{2,0,1:T(8,128)(2,1)S(1)} async-done(((bf16[128,32,128]{2,0,1:T(8,128)(2,1)}), bf16[128,32,128]{2,0,1:T(8,128)(2,1)S(1)}, u32[]{:S(2)}, u32[]{:S(2)}) %all-to-all-start.1) | async-done | bytes 1048608 | tf_op jit(solution)/shard_map/all_to_all | solution.py:92
  49.7 4.2 %all-to-all-start.2 = ((bf16[128,32,128]{2,0,1:T(8,128)(2,1)}), bf16[128,32,128]{2,0,1:T(8,128)(2,1)}, u32[]{:S(2)}, u32[]{:S(2)}) async-start(bf16[128,32,128]{2,0,1:T(8,128)(2,1)} %copy.101), calls=%async_computation.2 | async-start | bytes 2097152 | tf_op jit(solution)/shard_map/all_to_all | solution.py:85
  56.6 11.8 %all-to-all-done.2 = bf16[128,32,128]{2,0,1:T(8,128)(2,1)} async-done(((bf16[128,32,128]{2,0,1:T(8,128)(2,1)}), bf16[128,32,128]{2,0,1:T(8,128)(2,1)}, u32[]{:S(2)}, u32[]{:S(2)}) %all-to-all-start.2) | async-done | bytes 1048608 | tf_op jit(solution)/shard_map/all_to_all | solution.py:85
  69.8 7.5 %fusion.20 = (f32[8,512]{1,0:T(8,128)S(1)}, f32[8,512,512]{1,2,0:T(8,128)}) fusion(pred[512,512]{0,1:T(8,128)(4,1)S(1)} %fusion.15, bf16[512,8,128]{2,0,1:T(8,128)(2,1)S(1)} %bitcast.96, bf16[512,8,128]{2,0,1:T(8,128)(2,1)} %bitcast.98), kind=kOutput, calls=%fused_computation.34 | convolution fusion | flops 545260032 | bytes 10764288 | tf_op jit(solution)/shard_map/sub | solution.py:41
  77.3 4.6 %fusion.7 = bf16[8,512,512]{1,2,0:T(8,128)(2,1)S(1)} fusion(f32[8,512,512]{1,2,0:T(8,128)} %get-tuple-element.69, f32[8,512]{1,0:T(8,128)S(1)} %get-tuple-element.68), kind=kLoop, calls=%fused_computation.13 | loop fusion | flops 4194304 | bytes 12599296 | tf_op jit(solution)/shard_map/convert_element_type | solution.py:43
  83.9 16.9 %all_to_all.105 = bf16[512,8,128]{2,1,0:T(8,128)(2,1)S(1)} all-to-all(bf16[512,8,128]{2,1,0:T(8,128)(2,1)S(1)} %copy.104), channel_id=1, replica_groups=mesh['dp'=8,'seq'=4] {'seq'}, dimensions={0} | all-to-all | bytes 2097152 | tf_op jit(solution)/shard_map/all_to_all | solution.py:112
  101.6 4.5 %convolution_bitcast_fusion = f32[4096,512]{0,1:T(8,128)} fusion(bf16[128,512]{0,1:T(8,128)(2,1)S(1)} %bitcast.94, bf16[1,128,4096]{2,1,0:T(8,128)(2,1)S(1)} %copy-done), kind=kOutput, calls=%fused_computation.5 | convolution fusion | flops 536870912 | bytes 9568256 | tf_op jit(solution)/shard_map/tr,tc->rc/dot_general | solution.py:128
  106.2 3.1 %fusion.12 = bf16[16,4,8,128]{3,2,1,0:T(8,128)(2,1)S(1)} fusion(bf16[4096,512]{1,0:T(8,128)(2,1)} %all-gather.2.cloned.1.call-done, bf16[1,128,4096]{2,1,0:T(8,128)(2,1)S(1)} %copy-done), kind=kOutput, calls=%fused_computation.23 | convolution fusion | flops 536936448 | bytes 5373952 | tf_op jit(solution)/shard_map/dot_general | solution.py:76
  109.5 28.8 %all_to_all.106 = bf16[128,32,128]{2,0,1:T(8,128)(2,1)S(1)} all-to-all(bf16[128,32,128]{2,0,1:T(8,128)(2,1)S(1)} %bitcast.85), channel_id=1, replica_groups=mesh['dp'=8,'seq'=4] {'seq'}, dimensions={1} | all-to-all | bytes 2097152 | tf_op jit(solution)/shard_map/all_to_all | solution.py:99
  140.2 4.8 %fusion.1 = bf16[8,512,512]{1,2,0:T(8,128)(2,1)S(1)} fusion(f32[8,512]{1,0:T(8,128)S(1)} %bitcast.104, f32[8,512,512]{1,2,0:T(8,128)} %get-tuple-element.69, f32[8,512]{1,0:T(8,128)S(1)} %get-tuple-element.68, bf16[512,8,128]{2,0,1:T(8,128)(2,1)S(1)} %bitcast.93, bf16[512,8,128]{2,0,1:T(8,128)(2,1)S(1)} %bitcast.91), kind=kOutput, calls=%fused_computation.2 | convolution fusion | flops 545259520 | bytes 14712832 | tf_op jit(solution)/shard_map/ihd,jhd->hij/dot_general | solution.py:48
  148.6 3.5 %all-to-all-start.5 = ((bf16[512,8,128]{2,1,0:T(8,128)(2,1)}), bf16[512,8,128]{2,1,0:T(8,128)(2,1)S(1)}, u32[]{:S(2)}, u32[]{:S(2)}) async-start(bf16[512,8,128]{2,1,0:T(8,128)(2,1)} %copy.113), calls=%async_computation.5 | async-start | bytes 2097152 | tf_op jit(solution)/shard_map/all_to_all | solution.py:118
  152.1 3.5 %fusion.11 = bf16[512,8,128]{2,0,1:T(8,128)(2,1)S(1)} fusion(bf16[8,512,512]{1,2,0:T(8,128)(2,1)} %copy-done.8, bf16[512,8,128]{2,0,1:T(8,128)(2,1)S(1)} %bitcast.97), kind=kOutput, calls=%fused_computation.21 | convolution fusion | flops 537919488 | bytes 6291456 | tf_op jit(solution)/shard_map/hij,ihd->jhd/dot_general | solution.py:60
  157.4 21.1 %all-to-all-done.5 = bf16[512,8,128]{2,1,0:T(8,128)(2,1)S(1)} async-done(((bf16[512,8,128]{2,1,0:T(8,128)(2,1)}), bf16[512,8,128]{2,1,0:T(8,128)(2,1)S(1)}, u32[]{:S(2)}, u32[]{:S(2)}) %all-to-all-start.5) | async-done | bytes 1048608 | tf_op jit(solution)/shard_map/all_to_all | solution.py:118
  178.4 3.5 %all-to-all-start.6 = ((bf16[512,8,128]{2,1,0:T(8,128)(2,1)}), bf16[512,8,128]{2,1,0:T(8,128)(2,1)S(1)}, u32[]{:S(2)}, u32[]{:S(2)}) async-start(bf16[512,8,128]{2,1,0:T(8,128)(2,1)} %copy.115), calls=%async_computation.6 | async-start | bytes 2097152 | tf_op jit(solution)/shard_map/all_to_all | solution.py:109
  181.9 4.7 %fusion.3 = bf16[1,128,4096]{2,1,0:T(8,128)(2,1)} fusion(bf16[128,512]{0,1:T(8,128)(2,1)S(1)} %bitcast.95, bf16[4096,512]{1,0:T(8,128)(2,1)} %all-gather.2.cloned.1.call-done), kind=kOutput, calls=%fused_computation.8 | convolution fusion | flops 537395200 | bytes 5373952 | tf_op jit(solution)/shard_map/tc,rc->tr/dot_general | solution.py:120
  187.8 2.3 broadcast_in_dim_reshape.3
  190.1 18.4 %all-to-all-done.6 = bf16[512,8,128]{2,1,0:T(8,128)(2,1)S(1)} async-done(((bf16[512,8,128]{2,1,0:T(8,128)(2,1)}), bf16[512,8,128]{2,1,0:T(8,128)(2,1)S(1)}, u32[]{:S(2)}, u32[]{:S(2)}) %all-to-all-start.6) | async-done | bytes 1048608 | tf_op jit(solution)/shard_map/all_to_all | solution.py:109
  210.1 51.2 %reduce-scatter.2.cloned.1.call-done = f32[128,512]{0,1:T(8,128)} async-done(((f32[4096,512]{0,1:T(8,128)}), f32[128,512]{0,1:T(8,128)}) %reduce-scatter.2.cloned.1.call-update) | async-done | bytes 262160 | tf_op jit(solution)/shard_map/reduce_scatter | solution.py:127
  261.3 1.8 copy.118
  (51 shorter events, 21.9 us)
Async XLA Ops:
  8.0 93.6 %copy-start = (bf16[1,128,4096]{2,1,0:T(8,128)(2,1)S(1)}, bf16[1,128,4096]{2,1,0:T(8,128)(2,1)}, u32[]{:S(2)}) copy-start(bf16[1,128,4096]{2,1,0:T(8,128)(2,1)} %param.14) | copy-start | bytes 3145732
  8.0 7.9 %copy-start.6 = (bf16[1,128,512]{2,1,0:T(8,128)(2,1)S(1)}, bf16[1,128,512]{2,1,0:T(8,128)(2,1)}, u32[]{:S(2)}) copy-start(bf16[1,128,512]{2,1,0:T(8,128)(2,1)} %param.16) | copy-start | bytes 393220
  8.0 98.1 %all-gather.2.cloned.1.call-start = ((), (), s32[]{:S(2)}) async-start(), calls=%async_computation.8 | async-start | bytes 4718592 | tf_op jit(solution)/shard_map/all_gather | solution.py:123
  11.7 18.7 %all-to-all-start = ((bf16[128,32,128]{2,0,1:T(8,128)(2,1)}), bf16[128,32,128]{2,0,1:T(8,128)(2,1)S(1)}, u32[]{:S(2)}, u32[]{:S(2)}) async-start(bf16[128,32,128]{2,0,1:T(8,128)(2,1)} %copy.94), calls=%async_computation | async-start | bytes 2097152 | tf_op jit(solution)/shard_map/all_to_all | solution.py:84
  31.6 22.4 %copy-start.7 = (s32[1,16]{1,0:T(1,128)S(1)}, s32[1,16]{1,0:T(1,128)}, u32[]{:S(2)}) copy-start(s32[1,16]{1,0:T(1,128)} %param.18) | copy-start | bytes 196
  31.6 18.1 %all-to-all-start.1 = ((bf16[128,32,128]{2,0,1:T(8,128)(2,1)}), bf16[128,32,128]{2,0,1:T(8,128)(2,1)S(1)}, u32[]{:S(2)}, u32[]{:S(2)}) async-start(bf16[128,32,128]{2,0,1:T(8,128)(2,1)} %bitcast.84), calls=%async_computation.1 | async-start | bytes 2097152 | tf_op jit(solution)/shard_map/all_to_all | solution.py:92
  49.7 18.8 %all-to-all-start.2 = ((bf16[128,32,128]{2,0,1:T(8,128)(2,1)}), bf16[128,32,128]{2,0,1:T(8,128)(2,1)}, u32[]{:S(2)}, u32[]{:S(2)}) async-start(bf16[128,32,128]{2,0,1:T(8,128)(2,1)} %copy.101), calls=%async_computation.2 | async-start | bytes 2097152 | tf_op jit(solution)/shard_map/all_to_all | solution.py:85
  53.9 207.4 %reduce-scatter.2.cloned.1.call-start = ((), (), s32[]{:S(2)}) async-start(), calls=%async_computation.9 | async-start | bytes 8650752 | tf_op jit(solution)/shard_map/reduce_scatter | solution.py:127
  55.6 14.2 %copy-start.3 = (bf16[4,128,8,128]{3,1,0,2:T(8,128)(2,1)S(1)}, bf16[4,128,8,128]{3,1,0,2:T(8,128)(2,1)}, u32[]{:S(2)}) copy-start(bf16[4,128,8,128]{3,1,0,2:T(8,128)(2,1)} %copy.96) | copy-start | bytes 3145732
  81.9 2.0 copy-start.1
  106.1 32.2 %copy-start.2 = (bf16[8,512,512]{1,2,0:T(8,128)(2,1)S(1)}, bf16[8,512,512]{1,2,0:T(8,128)(2,1)}, u32[]{:S(2)}) copy-start(bf16[8,512,512]{1,2,0:T(8,128)(2,1)} %copy-done.1) | copy-start | bytes 12582916
  140.2 4.8 %copy-start.5 = (bf16[4,128,8,128]{3,1,0,2:T(8,128)(2,1)S(1)}, bf16[4,128,8,128]{3,1,0,2:T(8,128)(2,1)}, u32[]{:S(2)}) copy-start(bf16[4,128,8,128]{3,1,0,2:T(8,128)(2,1)} %copy.99) | copy-start | bytes 3145732
  145.0 2.0 copy-start.8
  145.0 7.1 %copy-start.4 = (bf16[4,128,8,128]{3,1,0,2:T(8,128)(2,1)S(1)}, bf16[4,128,8,128]{3,1,0,2:T(8,128)(2,1)}, u32[]{:S(2)}) copy-start(bf16[4,128,8,128]{3,1,0,2:T(8,128)(2,1)} %copy.96) | copy-start | bytes 3145732
  148.6 29.8 %all-to-all-start.5 = ((bf16[512,8,128]{2,1,0:T(8,128)(2,1)}), bf16[512,8,128]{2,1,0:T(8,128)(2,1)S(1)}, u32[]{:S(2)}, u32[]{:S(2)}) async-start(bf16[512,8,128]{2,1,0:T(8,128)(2,1)} %copy.113), calls=%async_computation.5 | async-start | bytes 2097152 | tf_op jit(solution)/shard_map/all_to_all | solution.py:118
  178.4 30.1 %all-to-all-start.6 = ((bf16[512,8,128]{2,1,0:T(8,128)(2,1)}), bf16[512,8,128]{2,1,0:T(8,128)(2,1)S(1)}, u32[]{:S(2)}, u32[]{:S(2)}) async-start(bf16[512,8,128]{2,1,0:T(8,128)(2,1)} %copy.115), calls=%async_computation.6 | async-start | bytes 2097152 | tf_op jit(solution)/shard_map/all_to_all | solution.py:109
Sparse Core Ops, SparseCore 0:
  11.0 76.0 all-gather.1
Sparse Core Ops, SparseCore 1:
  106.2 155.1 reduce-scatter.1
where the time goes:
time: 271 us
  waiting for transfers between devices  127 us (47%)
  blocking collectives  45.7 us (17%)
  matrix products  32.6 us (12%)
  local copies, waits for them, and re-layouts  23.3 us (9%)
  starting transfers between devices  19.2 us (7%)
  between operations  15.8 us (6%)
  other arithmetic  6.44 us (2%)
    reduce_scatter x1, waiting for transfers between devices, body(): lax.psum_scatter(jnp.einsum('tr,tc->rc', columns, value_low, preferred_el...  51.2 us
    all_to_all x1, blocking collectives, body(): lax.all_to_all(jnp.repeat(value_three, group_size, axis=1), 'seq', split_...  28.8 us
    all_to_all x1, waiting for transfers between devices, body(): lax.all_to_all(query_back, 'seq', split_axis=0, concat_axis=1, tiled=True)  21.1 us
    all_to_all x1, waiting for transfers between devices, body(): lax.all_to_all(key_back.astype(jnp.bfloat16), 'seq', split_axis=0, concat...  18.4 us
    all_to_all x1, blocking collectives, body(): lax.all_to_all(value_back.astype(jnp.bfloat16), 'seq', split_axis=0, conc...  16.9 us
    all_to_all x1, waiting for transfers between devices, body(): lax.all_to_all(query_heads, 'seq', split_axis=1, concat_axis=0, tiled=True)  14.4 us
    all_to_all x1, waiting for transfers between devices, body(): lax.all_to_all(grad_heads, 'seq', split_axis=1, concat_axis=0, tiled=True)  11.8 us
    all_to_all x1, waiting for transfers between devices, body(): lax.all_to_all(jnp.repeat(key_three, group_size, axis=1), 'seq', split_ax...  9.88 us
  transfers between devices with their start and end apart: 7, of which 6 were waited for; matrix products, arithmetic and copies ran while one was open for 22% of the time, Pallas kernels for 0%

commit v1 on v0

--- a/solution.py
+++ b/solution.py
@@ -5,6 +5,22 @@
 
 HD = 128
 far_negative = -1e30
+
+
+def exchange_in_pairs(shard, axis, split, join):
+    ways, here = (lax.axis_size(axis), lax.axis_index(axis))
+    width = shard.shape[split] // ways
+    shape = list(shard.shape)
+    shape[split] = width
+    height = shape[join]
+    shape[join] = height * ways
+    full = jnp.zeros(shape, shard.dtype)
+    for mask in range(ways):
+        part = lax.dynamic_slice_in_dim(shard, (here ^ mask) * width, width, axis=split)
+        if mask:
+            part = lax.ppermute(part, axis, [(d, d ^ mask) for d in range(ways)])
+        full = lax.dynamic_update_slice_in_dim(full, part, (here ^ mask) * height, axis=join)
+    return full
 
 
 def segment_ids(lengths_row, length):
@@ -89,13 +105,7 @@
     value_three = values.reshape(tokens, kv_heads, HD)
     segment = segment_ids(doc_lengths[0], length)
     key_all, value_all = (
-        lax.all_to_all(
-            jnp.repeat(key_three, group_size, axis=1),
-            "seq",
-            split_axis=1,
-            concat_axis=0,
-            tiled=True,
-        ),
+        exchange_in_pairs(jnp.repeat(key_three, group_size, axis=1), "seq", 1, 0),
         lax.all_to_all(
             jnp.repeat(value_three, group_size, axis=1),
             "seq",

time: 271 us -> 263 us (0.970)
  waiting for transfers between devices: 127 us -> 118 us
    ppermute x0 -> x3, waiting for transfers between devices: none -> 16.2 us  [exchange_in_pairs(): part = lax.ppermute(part, axis, [(d, d ^ mask) for d in range(ways)])]
    all_to_all x1, waiting for transfers between devices: 11.8 us -> 0.01 us  [body(): lax.all_to_all(grad_heads, 'seq', split_axis=1, concat_axis=0, tiled=True)]
    all_to_all x1 -> x0, waiting for transfers between devices: 9.88 us -> none  [body(): lax.all_to_all(jnp.repeat(key_three, group_size, axis=1), 'seq', split_ax...]
    dynamic_update_slice x0 -> x3, local copies, waits for them, and re-layouts: none -> 4.07 us  [exchange_in_pairs(): lax.dynamic_update_slice_in_dim(full, part, (here ^ mask) * height, axis=...]
    all_to_all x1 -> x0, starting transfers between devices: 3.65 us -> none  [body(): lax.all_to_all(jnp.repeat(key_three, group_size, axis=1), 'seq', split_ax...]
    all_to_all x1, waiting for transfers between devices: 14.4 us -> 11.4 us  [body(): lax.all_to_all(query_heads, 'seq', split_axis=1, concat_axis=0, tiled=True)]
    unnamed x22 -> x28, local copies, waits for them, and re-layouts: 6.92 us -> 8.74 us
  transfers between devices with their start and end apart: 7 -> 9, of which waited for: 6 -> 6; matrix products, arithmetic and copies ran while one was open for 22% -> 23% of each run, Pallas kernels for 0% -> 0%
where the time goes in v1:
time: 263 us; the launch traced here: 262 us
  waiting for transfers between devices  118 us (45%)
  blocking collectives  45.7 us (17%)
  matrix products  32.6 us (12%)
  local copies, waits for them, and re-layouts  25.9 us (10%)
  starting transfers between devices  17 us (6%)
  between operations  15.8 us (6%)
  other arithmetic  7.15 us (3%)
    reduce_scatter x1, waiting for transfers between devices, body(): lax.psum_scatter(jnp.einsum('tr,tc->rc', columns, value_low, preferred_el...  51.4 us
    all_to_all x1, blocking collectives, body(): lax.all_to_all(jnp.repeat(value_three, group_size, axis=1), 'seq', split_...  28.8 us
    all_to_all x1, waiting for transfers between devices, body(): lax.all_to_all(query_back, 'seq', split_axis=0, concat_axis=1, tiled=True)  20.4 us
    all_to_all x1, waiting for transfers between devices, body(): lax.all_to_all(key_back.astype(jnp.bfloat16), 'seq', split_axis=0, concat...  18.1 us
    all_to_all x1, blocking collectives, body(): lax.all_to_all(value_back.astype(jnp.bfloat16), 'seq', split_axis=0, conc...  16.9 us
    ppermute x3, waiting for transfers between devices, exchange_in_pairs(): part = lax.ppermute(part, axis, [(d, d ^ mask) for d in range(ways)])  16.2 us
    all_to_all x1, waiting for transfers between devices, body(): lax.all_to_all(query_heads, 'seq', split_axis=1, concat_axis=0, tiled=True)  11.4 us
    unnamed x28, local copies, waits for them, and re-layouts  8.74 us
  transfers between devices with their start and end apart: 9, of which 6 were waited for; matrix products, arithmetic and copies ran while one was open for 23% of the time, Pallas kernels for 0%

profile of v1, /device:TPU:0, one launch (start us, length us, event | category | flops | bytes accessed | tf_op | source)
XLA Modules:
  0.0 262.3 jit_solution(9439346386992776012)
XLA Ops:
  11.7 4.2 %all-to-all-start = ((bf16[128,32,128]{2,0,1:T(8,128)(2,1)}), bf16[128,32,128]{2,0,1:T(8,128)(2,1)S(1)}, u32[]{:S(2)}, u32[]{:S(2)}) async-start(bf16[128,32,128]{2,0,1:T(8,128)(2,1)} %copy.97), calls=%async_computation | async-start | bytes 2097152 | tf_op jit(solution)/shard_map/all_to_all | solution.py:100
  19.0 11.4 %all-to-all-done = bf16[128,32,128]{2,0,1:T(8,128)(2,1)S(1)} async-done(((bf16[128,32,128]{2,0,1:T(8,128)(2,1)}), bf16[128,32,128]{2,0,1:T(8,128)(2,1)S(1)}, u32[]{:S(2)}, u32[]{:S(2)}) %all-to-all-start) | async-done | bytes 1048608 | tf_op jit(solution)/shard_map/all_to_all | solution.py:100
  30.4 3.5 %all-to-all-start.1 = ((bf16[128,32,128]{2,0,1:T(8,128)(2,1)}), bf16[128,32,128]{2,0,1:T(8,128)(2,1)S(1)}, u32[]{:S(2)}, u32[]{:S(2)}) async-start(bf16[128,32,128]{2,0,1:T(8,128)(2,1)} %copy.102), calls=%async_computation.1 | async-start | bytes 2097152 | tf_op jit(solution)/shard_map/all_to_all | solution.py:101
  41.2 13.3 %collective-permute-done.1 = bf16[128,8,128]{0,2,1:T(8,128)(2,1)} collective-permute-done((bf16[128,8,128]{0,2,1:T(8,128)(2,1)}, bf16[128,8,128]{0,2,1:T(8,128)(2,1)}, u32[]{:S(2)}, u32[]{:S(2)}) %collective-permute-start.1) | collective-permute-done | bytes 262176 | tf_op jit(solution)/shard_map/ppermute | solution.py:21
  56.2 2.9 %collective-permute-done.2 = bf16[128,8,128]{0,2,1:T(8,128)(2,1)S(1)} collective-permute-done((bf16[128,8,128]{0,2,1:T(8,128)(2,1)}, bf16[128,8,128]{0,2,1:T(8,128)(2,1)S(1)}, u32[]{:S(2)}, u32[]{:S(2)}) %collective-permute-start.2) | collective-permute-done | bytes 262176 | tf_op jit(solution)/shard_map/ppermute | solution.py:21
  61.0 8.3 %fusion.20 = (f32[8,512]{1,0:T(8,128)S(1)}, f32[8,512,512]{1,2,0:T(8,128)}) fusion(pred[512,512]{0,1:T(8,128)(4,1)S(1)} %copy-done.9, bf16[512,8,128]{0,2,1:T(8,128)(2,1)} %constant_dynamic-update-slice_fusion, bf16[512,8,128]{2,0,1:T(8,128)(2,1)} %bitcast.104), kind=kOutput, calls=%fused_computation.41 | convolution fusion | flops 545260032 | bytes 10764288 | tf_op jit(solution)/shard_map/sub | solution.py:57
  69.3 4.6 %fusion.7 = bf16[8,512,512]{1,2,0:T(8,128)(2,1)S(1)} fusion(f32[8,512,512]{1,2,0:T(8,128)} %get-tuple-element.73, f32[8,512]{1,0:T(8,128)S(1)} %get-tuple-element.72), kind=kLoop, calls=%fused_computation.13 | loop fusion | flops 4194304 | bytes 12599296 | tf_op jit(solution)/shard_map/convert_element_type | solution.py:59
  75.9 16.9 %all_to_all.87 = bf16[512,8,128]{2,1,0:T(8,128)(2,1)S(1)} all-to-all(bf16[512,8,128]{2,1,0:T(8,128)(2,1)S(1)} %copy.105), channel_id=1, replica_groups=mesh['dp'=8,'seq'=4] {'seq'}, dimensions={0} | all-to-all | bytes 2097152 | tf_op jit(solution)/shard_map/all_to_all | solution.py:122
  93.6 4.5 %convolution_bitcast_fusion = f32[4096,512]{0,1:T(8,128)} fusion(bf16[128,512]{0,1:T(8,128)(2,1)S(1)} %bitcast.102, bf16[1,128,4096]{2,1,0:T(8,128)(2,1)S(1)} %copy-done), kind=kOutput, calls=%fused_computation.5 | convolution fusion | flops 536870912 | bytes 9568256 | tf_op jit(solution)/shard_map/tr,tc->rc/dot_general | solution.py:138
  98.2 3.1 %fusion.12 = bf16[16,4,8,128]{3,2,1,0:T(8,128)(2,1)S(1)} fusion(bf16[4096,512]{1,0:T(8,128)(2,1)} %all-gather.2.cloned.1.call-done, bf16[1,128,4096]{2,1,0:T(8,128)(2,1)S(1)} %copy-done), kind=kOutput, calls=%fused_computation.23 | convolution fusion | flops 536936448 | bytes 5373952 | tf_op jit(solution)/shard_map/dot_general | solution.py:92
  101.5 28.8 %all_to_all.88 = bf16[128,32,128]{2,0,1:T(8,128)(2,1)S(1)} all-to-all(bf16[128,32,128]{2,0,1:T(8,128)(2,1)S(1)} %bitcast.93), channel_id=1, replica_groups=mesh['dp'=8,'seq'=4] {'seq'}, dimensions={1} | all-to-all | bytes 2097152 | tf_op jit(solution)/shard_map/all_to_all | solution.py:109
  130.4 1.8 fusion.8
  132.2 4.8 %fusion.1 = bf16[8,512,512]{1,2,0:T(8,128)(2,1)S(1)} fusion(f32[8,512]{1,0:T(8,128)S(1)} %bitcast.111, f32[8,512,512]{1,2,0:T(8,128)} %get-tuple-element.73, f32[8,512]{1,0:T(8,128)S(1)} %get-tuple-element.72, bf16[512,8,128]{2,0,1:T(8,128)(2,1)S(1)} %bitcast.101, bf16[512,8,128]{2,0,1:T(8,128)(2,1)S(1)} %bitcast.99), kind=kOutput, calls=%fused_computation.2 | convolution fusion | flops 545259520 | bytes 14712832 | tf_op jit(solution)/shard_map/ihd,jhd->hij/dot_general | solution.py:64
  137.0 1.9 copy-done.3
  141.1 3.5 %all-to-all-start.4 = ((bf16[512,8,128]{2,1,0:T(8,128)(2,1)}), bf16[512,8,128]{2,1,0:T(8,128)(2,1)S(1)}, u32[]{:S(2)}, u32[]{:S(2)}) async-start(bf16[512,8,128]{2,1,0:T(8,128)(2,1)} %copy.114), calls=%async_computation.4 | async-start | bytes 2097152 | tf_op jit(solution)/shard_map/all_to_all | solution.py:128
  144.7 3.5 %fusion.11 = bf16[512,8,128]{2,0,1:T(8,128)(2,1)S(1)} fusion(bf16[8,512,512]{1,2,0:T(8,128)(2,1)} %copy-done.3, bf16[512,8,128]{2,0,1:T(8,128)(2,1)S(1)} %bitcast.105), kind=kOutput, calls=%fused_computation.21 | convolution fusion | flops 537919488 | bytes 6291456 | tf_op jit(solution)/shard_map/hij,ihd->jhd/dot_general | solution.py:76
  148.2 1.7 copy.116
  149.9 20.4 %all-to-all-done.4 = bf16[512,8,128]{2,1,0:T(8,128)(2,1)S(1)} async-done(((bf16[512,8,128]{2,1,0:T(8,128)(2,1)}), bf16[512,8,128]{2,1,0:T(8,128)(2,1)S(1)}, u32[]{:S(2)}, u32[]{:S(2)}) %all-to-all-start.4) | async-done | bytes 1048608 | tf_op jit(solution)/shard_map/all_to_all | solution.py:128
  170.3 3.5 %all-to-all-start.5 = ((bf16[512,8,128]{2,1,0:T(8,128)(2,1)}), bf16[512,8,128]{2,1,0:T(8,128)(2,1)S(1)}, u32[]{:S(2)}, u32[]{:S(2)}) async-start(bf16[512,8,128]{2,1,0:T(8,128)(2,1)} %copy.116), calls=%async_computation.5 | async-start | bytes 2097152 | tf_op jit(solution)/shard_map/all_to_all | solution.py:119
  173.8 4.7 %fusion.3 = bf16[1,128,4096]{2,1,0:T(8,128)(2,1)} fusion(bf16[128,512]{0,1:T(8,128)(2,1)S(1)} %bitcast.103, bf16[4096,512]{1,0:T(8,128)(2,1)} %all-gather.2.cloned.1.call-done), kind=kOutput, calls=%fused_computation.8 | convolution fusion | flops 537395200 | bytes 5373952 | tf_op jit(solution)/shard_map/tc,rc->tr/dot_general | solution.py:130
  179.7 2.3 broadcast_in_dim_reshape.3
  182.0 18.1 %all-to-all-done.5 = bf16[512,8,128]{2,1,0:T(8,128)(2,1)S(1)} async-done(((bf16[512,8,128]{2,1,0:T(8,128)(2,1)}), bf16[512,8,128]{2,1,0:T(8,128)(2,1)S(1)}, u32[]{:S(2)}, u32[]{:S(2)}) %all-to-all-start.5) | async-done | bytes 1048608 | tf_op jit(solution)/shard_map/all_to_all | solution.py:119
  201.6 51.4 %reduce-scatter.2.cloned.1.call-done = f32[128,512]{0,1:T(8,128)} async-done(((f32[4096,512]{0,1:T(8,128)}), f32[128,512]{0,1:T(8,128)}) %reduce-scatter.2.cloned.1.call-update) | async-done | bytes 262160 | tf_op jit(solution)/shard_map/reduce_scatter | solution.py:137
  253.1 1.8 copy.119
  (64 shorter events, 25.6 us)
Async XLA Ops:
  8.0 85.6 %copy-start = (bf16[1,128,4096]{2,1,0:T(8,128)(2,1)S(1)}, bf16[1,128,4096]{2,1,0:T(8,128)(2,1)}, u32[]{:S(2)}) copy-start(bf16[1,128,4096]{2,1,0:T(8,128)(2,1)} %param.14) | copy-start | bytes 3145732
  8.0 7.9 %copy-start.10 = (bf16[1,128,512]{2,1,0:T(8,128)(2,1)S(1)}, bf16[1,128,512]{2,1,0:T(8,128)(2,1)}, u32[]{:S(2)}) copy-start(bf16[1,128,512]{2,1,0:T(8,128)(2,1)} %param.16) | copy-start | bytes 393220
  8.0 90.1 %all-gather.2.cloned.1.call-start = ((), (), s32[]{:S(2)}) async-start(), calls=%async_computation.7 | async-start | bytes 4718592 | tf_op jit(solution)/shard_map/all_gather | solution.py:133
  11.7 18.7 %all-to-all-start = ((bf16[128,32,128]{2,0,1:T(8,128)(2,1)}), bf16[128,32,128]{2,0,1:T(8,128)(2,1)S(1)}, u32[]{:S(2)}, u32[]{:S(2)}) async-start(bf16[128,32,128]{2,0,1:T(8,128)(2,1)} %copy.97), calls=%async_computation | async-start | bytes 2097152 | tf_op jit(solution)/shard_map/all_to_all | solution.py:100
  17.7 20.6 %copy-start.11 = (s32[1,16]{1,0:T(1,128)S(1)}, s32[1,16]{1,0:T(1,128)}, u32[]{:S(2)}) copy-start(s32[1,16]{1,0:T(1,128)} %param.18) | copy-start | bytes 196
  30.4 30.5 %all-to-all-start.1 = ((bf16[128,32,128]{2,0,1:T(8,128)(2,1)}), bf16[128,32,128]{2,0,1:T(8,128)(2,1)S(1)}, u32[]{:S(2)}, u32[]{:S(2)}) async-start(bf16[128,32,128]{2,0,1:T(8,128)(2,1)} %copy.102), calls=%async_computation.1 | async-start | bytes 2097152 | tf_op jit(solution)/shard_map/all_to_all | solution.py:101
  33.9 219.1 %reduce-scatter.2.cloned.1.call-start = ((), (), s32[]{:S(2)}) async-start(), calls=%async_computation.8 | async-start | bytes 8650752 | tf_op jit(solution)/shard_map/reduce_scatter | solution.py:137
  35.2 1.0 copy-start.6
  36.2 3.4 %collective-permute-start = (bf16[128,8,128]{0,2,1:T(8,128)(2,1)}, bf16[128,8,128]{0,2,1:T(8,128)(2,1)}, u32[]{:S(2)}, u32[]{:S(2)}) collective-permute-start(bf16[128,8,128]{0,2,1:T(8,128)(2,1)} %get-tuple-element.70), channel_id=1, source_target_pairs={{0,1},{1,0},{2,3},{3,2},{4,5},{5,4},{6,7},{7,6},{8,9},{9,8},{10,11... | collective-permute-start | bytes 786440 | tf_op jit(solution)/shard_map/ppermute | solution.py:21
  36.6 17.9 %collective-permute-start.1 = (bf16[128,8,128]{0,2,1:T(8,128)(2,1)}, bf16[128,8,128]{0,2,1:T(8,128)(2,1)}, u32[]{:S(2)}, u32[]{:S(2)}) collective-permute-start(bf16[128,8,128]{0,2,1:T(8,128)(2,1)} %get-tuple-element.69), channel_id=1, source_target_pairs={{0,2},{1,3},{2,0},{3,1},{4,6},{5,7},{6,4},{7,5},{8,10},{9,11},{10,... | collective-permute-start | bytes 786440 | tf_op jit(solution)/shard_map/ppermute | solution.py:21
  38.3 20.8 %collective-permute-start.2 = (bf16[128,8,128]{0,2,1:T(8,128)(2,1)}, bf16[128,8,128]{0,2,1:T(8,128)(2,1)S(1)}, u32[]{:S(2)}, u32[]{:S(2)}) collective-permute-start(bf16[128,8,128]{0,2,1:T(8,128)(2,1)} %get-tuple-element.68), channel_id=1, source_target_pairs={{0,3},{1,2},{2,1},{3,0},{4,7},{5,6},{6,5},{7,4},{8,11},{9,10},{10,... | collective-permute-start | bytes 786440 | tf_op jit(solution)/shard_map/ppermute | solution.py:21
  59.8 1.2 copy-start.9
  61.0 12.9 %copy-start.4 = (bf16[4,128,8,128]{3,1,0,2:T(8,128)(2,1)}, bf16[4,128,8,128]{3,1,0,2:T(8,128)(2,1)S(1)}, u32[]{:S(2)}) copy-start(bf16[4,128,8,128]{3,1,0,2:T(8,128)(2,1)S(1)} %copy.104) | copy-start | bytes 3145732
  73.9 2.0 copy-start.1
  98.1 32.3 %copy-start.5 = (bf16[4,128,8,128]{3,1,0,2:T(8,128)(2,1)S(1)}, bf16[4,128,8,128]{3,1,0,2:T(8,128)(2,1)}, u32[]{:S(2)}) copy-start(bf16[4,128,8,128]{3,1,0,2:T(8,128)(2,1)} %copy-done.4) | copy-start | bytes 3145732
  98.2 32.3 %copy-start.2 = (bf16[8,512,512]{1,2,0:T(8,128)(2,1)S(1)}, bf16[8,512,512]{1,2,0:T(8,128)(2,1)}, u32[]{:S(2)}) copy-start(bf16[8,512,512]{1,2,0:T(8,128)(2,1)} %copy-done.1) | copy-start | bytes 12582916
  132.2 6.7 %copy-start.7 = (bf16[512,8,128]{0,2,1:T(8,128)(2,1)S(1)}, bf16[512,8,128]{0,2,1:T(8,128)(2,1)}, u32[]{:S(2)}) copy-start(bf16[512,8,128]{0,2,1:T(8,128)(2,1)} %constant_dynamic-update-slice_fusion) | copy-start | bytes 3145732
  137.0 1.9 copy-start.3
  139.0 5.7 %copy-start.8 = (bf16[4,128,8,128]{3,1,0,2:T(8,128)(2,1)S(1)}, bf16[4,128,8,128]{3,1,0,2:T(8,128)(2,1)}, u32[]{:S(2)}) copy-start(bf16[4,128,8,128]{3,1,0,2:T(8,128)(2,1)} %copy.99) | copy-start | bytes 3145732
  141.1 29.1 %all-to-all-start.4 = ((bf16[512,8,128]{2,1,0:T(8,128)(2,1)}), bf16[512,8,128]{2,1,0:T(8,128)(2,1)S(1)}, u32[]{:S(2)}, u32[]{:S(2)}) async-start(bf16[512,8,128]{2,1,0:T(8,128)(2,1)} %copy.114), calls=%async_computation.4 | async-start | bytes 2097152 | tf_op jit(solution)/shard_map/all_to_all | solution.py:128
  170.3 29.7 %all-to-all-start.5 = ((bf16[512,8,128]{2,1,0:T(8,128)(2,1)}), bf16[512,8,128]{2,1,0:T(8,128)(2,1)S(1)}, u32[]{:S(2)}, u32[]{:S(2)}) async-start(bf16[512,8,128]{2,1,0:T(8,128)(2,1)} %copy.116), calls=%async_computation.5 | async-start | bytes 2097152 | tf_op jit(solution)/shard_map/all_to_all | solution.py:119
Sparse Core Ops, SparseCore 0:
  11.0 76.0 all-gather.1
Sparse Core Ops, SparseCore 1:
  98.2 154.8 reduce-scatter.1
